TPU v7x, 32 devices: a whole 2x2x4 slice. The times are simulated.
32 devices in a mesh: groups: 2 (over y), seq: 4 (over z), rep: 4 (over x, core).
Axes of the slice: x: 2, y: 2, z: 4, core: 2. Of those that a mesh axis runs over, the one named last changes fastest.
Arguments:
- hidden: bfloat16 [8, 512, 2048], P(('groups', 'rep'), 'seq'), parts along dimension 0, may hold values from -6 to 6
- shared_weight: bfloat16 [2048, 1024], P('seq'), may hold values from -0.125 to 0.125
- values: bfloat16 [8, 512, 1024], P(('groups', 'rep'), 'seq'), parts along dimension 0, may hold values from -6 to 6
- clusters: int32 [8, 512, 1], P(('groups', 'rep'), 'seq'), parts along dimension 0, may hold values from 0 to 7; in each aligned block of 128 rows (0 to 127, 128 to 255, ..., all dimensions but the last counted through in order) at most 32 rows name the same one
- cotangent: bfloat16 [8, 512, 1024], P(('groups', 'rep'), 'seq'), parts along dimension 0, may hold values from -6 to 6
Outputs:
- attended: bfloat16 [8, 512, 1024], P(('groups', 'rep'), 'seq'), parts along dimension 0
- hidden_grad: bfloat16 [8, 512, 2048], P(('groups', 'rep'), 'seq'), parts along dimension 0
- values_grad: bfloat16 [8, 512, 1024], P(('groups', 'rep'), 'seq'), parts along dimension 0
- weight_grad: float32 [4096, 1024], P(('groups', 'seq')), parts along dimension 0
There are 2 independent parts, one for each index of `groups`. A program takes and returns all parts, laid end to end along the dimension named above; an argument that names none is the same for every part. Nothing has to cross between parts.
Inputs may be any that keep to these rules, and one draw needn't show every extreme that they name: `clusters`: within each aligned block of 128 tokens of a sequence, no cluster id occurs more than 32 times, and in every draw some id occurs exactly 32 times in some block.
All inputs are finite; a program needn't handle non-finite values.
Results may differ from a plain program's by a relative error of at most 0.014.
Values may be sent and summed in bfloat16 or wider, within the bound.
A program may use at most 64 MiB of HBM per device.

v0:
```python
import jax
import jax.numpy as jnp
from jax import lax
from jax.sharding import PartitionSpec as P

HEADS = 8
HEAD_SIZE = 128
CL_DEV = 2


SOFTMAX_HEAT = 8.0
EPSILON = 1e-06


def attend_owned(received):
    q_recv, v_recv, g_recv, p_recv = received
    sources = q_recv.shape[0]
    items = q_recv.shape[1]
    slots = q_recv.shape[2]
    width = q_recv.shape[3]
    capacity = sources * slots

    def regroup(rows):
        return jnp.transpose(rows, (1, 0, 2, 3)).reshape(items, capacity, HEADS, HEAD_SIZE)

    query_four = regroup(q_recv)
    v_four = regroup(v_recv)
    g_four = regroup(g_recv)
    pos_items = jnp.transpose(p_recv, (1, 0, 2)).reshape(items, capacity)
    score_scale = SOFTMAX_HEAT / HEAD_SIZE
    scores = (
        jnp.einsum("nihd,njhd->nhij", query_four, query_four, preferred_element_type=jnp.float32)
        * score_scale
    )
    pos_row = pos_items[:, None, :, None]
    pos_col = pos_items[:, None, None, :]
    before = (pos_col < pos_row) & (pos_col >= 0)
    diagonal = jnp.eye(capacity, dtype=jnp.bool_)
    keep_mask = before | diagonal[None, None]
    score_logits = jnp.where(before, scores, 0.0)
    exponent_terms = jnp.where(keep_mask, jnp.exp(score_logits - SOFTMAX_HEAT), 0.0)
    probs = exponent_terms / jnp.sum(exponent_terms, -1, keepdims=True)
    probs_low = probs.astype(jnp.bfloat16)
    out_rows = jnp.einsum("nhij,njhd->nihd", probs_low, v_four, preferred_element_type=jnp.float32)
    dprob = jnp.einsum("nihd,njhd->nhij", g_four, v_four, preferred_element_type=jnp.float32)
    delta = jnp.sum(probs * dprob, -1, keepdims=True)
    dscore = jnp.where(before, probs * (dprob - delta), 0.0).astype(jnp.bfloat16)
    q_grad = score_scale * (
        jnp.einsum("nhij,njhd->nihd", dscore, query_four, preferred_element_type=jnp.float32)
        + jnp.einsum("nhji,njhd->nihd", dscore, query_four, preferred_element_type=jnp.float32)
    )
    v_grad = jnp.einsum("nhij,nihd->njhd", probs_low, g_four, preferred_element_type=jnp.float32)

    def restore(rows):
        shaped = rows.astype(jnp.bfloat16).reshape(items, sources, slots, width)
        return jnp.transpose(shaped, (1, 0, 2, 3))

    results = (restore(out_rows), restore(q_grad), restore(v_grad))
    return (
        lax.all_to_all(results[0], "seq", split_axis=0, concat_axis=0, tiled=True),
        lax.all_to_all(results[1], "seq", split_axis=0, concat_axis=0, tiled=True),
        lax.all_to_all(results[2], "seq", split_axis=0, concat_axis=0, tiled=True),
    )


def weight_rows(tokens, y_grad):
    summed = lax.psum_scatter(
        lax.dot_general(
            tokens, y_grad, (((0,), (0,)), ((), ())), preferred_element_type=jnp.float32
        ).astype(jnp.bfloat16),
        "seq",
        scatter_dimension=0,
        tiled=True,
    )
    return lax.psum(summed, "rep").astype(jnp.float32)


def input_grad(y_grad, weight_full):
    product = lax.dot_general(
        y_grad, weight_full, (((1,), (1,)), ((), ())), preferred_element_type=jnp.float32
    )
    return product.astype(jnp.bfloat16)


def local(hidden, shared_weight, values, clusters, cotangent):
    tokens = hidden[0]
    tok_count = tokens.shape[0]
    seq_count = lax.axis_size("seq")
    my_index = lax.axis_index("seq")
    n_clusters = CL_DEV * seq_count
    most = 2 * tok_count // n_clusters
    weight_full = lax.all_gather(shared_weight, "seq", axis=0, tiled=True)
    projected = jnp.dot(tokens, weight_full, preferred_element_type=jnp.float32)
    grouped = projected.reshape(tok_count, HEADS, HEAD_SIZE)
    inverse = lax.rsqrt(jnp.mean(grouped * grouped, -1, keepdims=True) + EPSILON)
    queries = (grouped * inverse).astype(jnp.bfloat16).reshape(tok_count, -1)
    width = queries.shape[1]
    cluster_ids = clusters[0, :, 0]
    one_hot = (cluster_ids[:, None] == jnp.arange(n_clusters, dtype=jnp.int32)[None, :]).astype(
        jnp.int32
    )
    rank = jnp.sum((jnp.cumsum(one_hot, 0) - one_hot) * one_hot, 1)
    slot = cluster_ids * most + rank
    n_slots = n_clusters * most

    def place(rows):
        filled = jnp.zeros((n_slots, width), jnp.bfloat16).at[slot].set(rows)
        return filled.reshape(seq_count, CL_DEV, most, width)

    positions = my_index * tok_count + jnp.arange(tok_count, dtype=jnp.int32)
    pos_send = (
        jnp.full((n_slots,), -1, jnp.int32).at[slot].set(positions).reshape(seq_count, CL_DEV, most)
    )
    back_att, back_q, back_v = attend_owned(
        (
            lax.all_to_all(place(queries), "seq", split_axis=0, concat_axis=0, tiled=True),
            lax.all_to_all(place(values[0]), "seq", split_axis=0, concat_axis=0, tiled=True),
            lax.all_to_all(place(cotangent[0]), "seq", split_axis=0, concat_axis=0, tiled=True),
            lax.all_to_all(pos_send, "seq", split_axis=0, concat_axis=0, tiled=True),
        )
    )
    attended = back_att.reshape(n_slots, width)[slot]
    q_tok = back_q.reshape(n_slots, width)[slot]
    v_tok = back_v.reshape(n_slots, width)[slot]
    dq = q_tok.astype(jnp.float32).reshape(tok_count, HEADS, HEAD_SIZE)
    dy = inverse * dq - grouped * inverse**3 * jnp.mean(dq * grouped, -1, keepdims=True)
    y_grad = dy.reshape(tok_count, width).astype(jnp.bfloat16)
    hidden_grad = input_grad(y_grad, weight_full)
    weight_grad = weight_rows(tokens, y_grad)
    return (attended[None], hidden_grad[None], v_tok[None], weight_grad)


def solution(mesh):
    placed = (
        P(("groups", "rep"), "seq", None),
        P("seq", None),
        P(("groups", "rep"), "seq", None),
        P(("groups", "rep"), "seq", None),
        P(("groups", "rep"), "seq", None),
    )
    return jax.shard_map(
        local,
        mesh=mesh,
        in_specs=placed,
        out_specs=(
            P(("groups", "rep"), "seq", None),
            P(("groups", "rep"), "seq", None),
            P(("groups", "rep"), "seq", None),
            P(("groups", "seq"), None),
        ),
        check_vma=False,
    )
```

profile of v0, /device:TPU:0, one launch (start us, length us, event | category | flops | bytes accessed | tf_op | source)
XLA Modules:
  0.0 326.6 jit_solution(3323712127824156824)
XLA Ops:
  12.0 6.3 %all-to-all-start.1 = ((s32[4,2,32]{2,1,0:T(2,128)}), s32[4,2,32]{2,1,0:T(2,128)S(1)}, u32[]{:S(2)}, u32[]{:S(2)}) async-start(s32[4,2,32]{2,1,0:T(2,128)} %reshape.140), calls=%async_computation.1 | async-start | bytes 8192 | tf_op jit(solution)/shard_map/all_to_all | solution.py:119
  18.3 2.4 scatter_custom_fusion
  20.7 3.2 all-to-all-done.1
  23.9 3.5 %all-to-all-start = ((bf16[4,2,32,1024]{3,2,1,0:T(8,128)(2,1)}), bf16[4,2,32,1024]{3,2,1,0:T(8,128)(2,1)S(1)}, u32[]{:S(2)}, u32[]{:S(2)}) async-start(bf16[4,2,32,1024]{3,2,1,0:T(8,128)(2,1)} %bitcast.5), calls=%async_computation | async-start | bytes 1048576 | tf_op jit(solution)/shard_map/all_to_all | solution.py:117
  27.4 2.4 scatter_custom_fusion.3
  29.8 74.4 %all-gather.2.cloned.1.call-done = bf16[2048,1024]{1,0:T(8,128)(2,1)} async-done(((bf16[512,1024]{1,0:T(8,128)(2,1)}), bf16[2048,1024]{1,0:T(8,128)(2,1)}) %all-gather.2.cloned.1.call-update) | async-done | bytes 4194320 | tf_op jit(solution)/shard_map/all_gather | solution.py:92
  104.2 6.5 %copy.81 = bf16[1024,2048]{1,0:T(8,128)(2,1)} copy(bf16[1024,2048]{0,1:T(8,128)(2,1)} %bitcast.88) | data formatting | bytes 8388608 | tf_op jit(solution)/shard_map/dot_general | solution.py:93
  110.7 3.5 %all-to-all-start.4 = ((bf16[4,2,32,1024]{3,2,1,0:T(8,128)(2,1)}), bf16[4,2,32,1024]{3,2,1,0:T(8,128)(2,1)S(1)}, u32[]{:S(2)}, u32[]{:S(2)}) async-start(bf16[4,2,32,1024]{3,2,1,0:T(8,128)(2,1)} %bitcast.20), calls=%async_computation.4 | async-start | bytes 1048576 | tf_op jit(solution)/shard_map/all_to_all | solution.py:118
  114.2 3.4 %multiply_reduce_fusion.2 = (f32[128,8]{0,1:T(8,128)S(1)}, f32[128,8,128]{0,2,1:T(8,128)S(1)}) fusion(bf16[8,128,2048]{2,1,0:T(8,128)(2,1)} %bitcast.89, bf16[1,128,2048]{2,1,0:T(8,128)(2,1)S(1)} %copy-done), kind=kOutput, calls=%fused_computation.42 | convolution fusion | flops 537132032 | bytes 5246976 | tf_op jit(solution)/shard_map/dot_general | solution.py:93
  117.9 2.0 scatter_custom_fusion.2
  119.8 9.1 %all-to-all-done.4 = bf16[4,2,32,1024]{3,2,1,0:T(8,128)(2,1)S(1)} async-done(((bf16[4,2,32,1024]{3,2,1,0:T(8,128)(2,1)}), bf16[4,2,32,1024]{3,2,1,0:T(8,128)(2,1)S(1)}, u32[]{:S(2)}, u32[]{:S(2)}) %all-to-all-start.4) | async-done | bytes 524320 | tf_op jit(solution)/shard_map/all_to_all | solution.py:118
  128.9 3.5 %all-to-all-start.2 = ((bf16[4,2,32,1024]{3,2,1,0:T(8,128)(2,1)}), bf16[4,2,32,1024]{3,2,1,0:T(8,128)(2,1)S(1)}, u32[]{:S(2)}, u32[]{:S(2)}) async-start(bf16[4,2,32,1024]{3,2,1,0:T(8,128)(2,1)} %bitcast.13), calls=%async_computation.2 | async-start | bytes 1048576 | tf_op jit(solution)/shard_map/all_to_all | solution.py:116
  133.4 1.3 fusion.30
  134.7 11.7 %all-to-all-done.2 = bf16[4,2,32,1024]{3,2,1,0:T(8,128)(2,1)S(1)} async-done(((bf16[4,2,32,1024]{3,2,1,0:T(8,128)(2,1)}), bf16[4,2,32,1024]{3,2,1,0:T(8,128)(2,1)S(1)}, u32[]{:S(2)}, u32[]{:S(2)}) %all-to-all-start.2) | async-done | bytes 524320 | tf_op jit(solution)/shard_map/all_to_all | solution.py:116
  148.4 1.1 fusion.24
  149.5 3.7 %fusion.15 = f32[2,8,128,128]{2,3,1,0:T(8,128)} fusion(bf16[2,128,8,128]{1,3,2,0:T(8,128)(2,1)S(1)} %copy.93, f32[2,8,128,128]{2,3,1,0:T(8,128)} %fusion.24, f32[2,8,128,128]{2,3,1,0:T(8,128)} %fusion.30, pred[2,128,128]{1,2,0:T(8,128)(4,1)S(1)} %get-tuple-element.23), kind=kOutput, calls=%fused_computation.28 | convolution fusion | flops 68421760 | bytes 3702784 | tf_op jit(solution)/shard_map/nhij,njhd->nihd/dot_general | solution.py:49
  153.2 3.9 %fusion.12 = bf16[2,128,8,128]{3,1,2,0:T(8,128)(2,1)} fusion(f32[2,8,128,128]{2,3,1,0:T(8,128)} %fusion.15, bf16[2,128,8,128]{1,3,2,0:T(8,128)(2,1)S(1)} %copy.93, f32[2,8,128,128]{2,3,1,0:T(8,128)} %fusion.24, f32[2,8,128,128]{2,3,1,0:T(8,128)} %fusion.30, pred[2,128,128]{1,2,0:T(8,128)(4,1)S(1)} %get-tuple-element.23), kind=kOutput, calls=%fused_computation.25 | convolution fusion | flops 69208192 | bytes 4227072 | tf_op jit(solution)/shard_map/nhji,njhd->nihd/dot_general | solution.py:50
  157.1 1.4 copy.99
  159.5 3.5 %all-to-all-start.5 = ((bf16[4,2,32,1024]{3,2,1,0:T(8,128)(2,1)}), bf16[4,2,32,1024]{3,2,1,0:T(8,128)(2,1)S(1)}, u32[]{:S(2)}, u32[]{:S(2)}) async-start(bf16[4,2,32,1024]{3,2,1,0:T(8,128)(2,1)} %copy.100), calls=%async_computation.5 | async-start | bytes 1048576 | tf_op jit(solution)/shard_map/all_to_all | solution.py:61
  163.3 13.7 %all-to-all-done.5 = bf16[4,2,32,1024]{3,2,1,0:T(8,128)(2,1)S(1)} async-done(((bf16[4,2,32,1024]{3,2,1,0:T(8,128)(2,1)}), bf16[4,2,32,1024]{3,2,1,0:T(8,128)(2,1)S(1)}, u32[]{:S(2)}, u32[]{:S(2)}) %all-to-all-start.5) | async-done | bytes 524320 | tf_op jit(solution)/shard_map/all_to_all | solution.py:61
  178.1 3.2 convert_bitcast_fusion
  181.4 2.0 fusion.13
  184.8 3.5 %all-to-all-start.3 = ((bf16[4,2,32,1024]{3,2,1,0:T(8,128)(2,1)}), bf16[4,2,32,1024]{3,2,1,0:T(8,128)(2,1)S(1)}, u32[]{:S(2)}, u32[]{:S(2)}) async-start(bf16[4,2,32,1024]{3,2,1,0:T(8,128)(2,1)} %copy.89), calls=%async_computation.3 | async-start | bytes 1048576 | tf_op jit(solution)/shard_map/all_to_all | solution.py:60
  188.3 2.1 fusion.14
  191.8 23.9 %all-to-all-done.3 = bf16[4,2,32,1024]{3,2,1,0:T(8,128)(2,1)S(1)} async-done(((bf16[4,2,32,1024]{3,2,1,0:T(8,128)(2,1)}), bf16[4,2,32,1024]{3,2,1,0:T(8,128)(2,1)S(1)}, u32[]{:S(2)}, u32[]{:S(2)}) %all-to-all-start.3) | async-done | bytes 524320 | tf_op jit(solution)/shard_map/all_to_all | solution.py:60
  215.7 7.3 %all-to-all-start.6 = ((bf16[4,2,32,1024]{3,2,1,0:T(8,128)(2,1)}), bf16[4,2,32,1024]{3,2,1,0:T(8,128)(2,1)S(1)}, u32[]{:S(2)}, u32[]{:S(2)}) async-start(bf16[4,2,32,1024]{3,2,1,0:T(8,128)(2,1)} %copy.105), calls=%async_computation.6 | async-start | bytes 1048576 | tf_op jit(solution)/shard_map/all_to_all | solution.py:62
  223.0 51.2 %reduce-scatter.2.cloned.1.call-done = bf16[512,1024]{0,1:T(8,128)(2,1)} async-done(((bf16[2048,1024]{0,1:T(8,128)(2,1)}), bf16[512,1024]{0,1:T(8,128)(2,1)}) %reduce-scatter.2.cloned.1.call-update) | async-done | bytes 1048592 | tf_op jit(solution)/shard_map/reduce_scatter | solution.py:67
  274.2 1.6 gather_fusion
  275.8 1.6 gather_fusion.2
  277.3 4.5 %fusion.1 = bf16[1,128,2048]{2,1,0:T(8,128)(2,1)} fusion(bf16[128,1024]{0,1:T(8,128)(2,1)S(1)} %bitcast.95, bf16[2048,1024]{1,0:T(8,128)(2,1)} %all-gather.2.cloned.1.call-done), kind=kOutput, calls=%fused_computation.10 | convolution fusion | flops 537133056 | bytes 4980736 | tf_op jit(solution)/shard_map/dot_general | solution.py:79
  281.8 35.7 %all-reduce.2.cloned.1.call-done = bf16[512,1024]{0,1:T(8,128)(2,1)} async-done(((bf16[512,1024]{0,1:T(8,128)(2,1)}), bf16[512,1024]{0,1:T(8,128)(2,1)}) %all-reduce.2.cloned.1.call-update) | async-done | bytes 1048592 | tf_op jit(solution)/shard_map/psum | solution.py:75
  317.5 2.6 copy.106
  (50 shorter events, 13.0 us)
Async XLA Ops:
  7.2 107.0 %copy-start = (bf16[1,128,2048]{2,1,0:T(8,128)(2,1)S(1)}, bf16[1,128,2048]{2,1,0:T(8,128)(2,1)}, u32[]{:S(2)}) copy-start(bf16[1,128,2048]{2,1,0:T(8,128)(2,1)} %param.5) | copy-start | bytes 1572868
  7.2 97.0 %all-gather.2.cloned.1.call-start = ((), (), s32[]{:S(2)}) async-start(), calls=%async_computation.8 | async-start | bytes 5242880 | tf_op jit(solution)/shard_map/all_gather | solution.py:92
  12.0 11.9 %all-to-all-start.1 = ((s32[4,2,32]{2,1,0:T(2,128)}), s32[4,2,32]{2,1,0:T(2,128)S(1)}, u32[]{:S(2)}, u32[]{:S(2)}) async-start(s32[4,2,32]{2,1,0:T(2,128)} %reshape.140), calls=%async_computation.1 | async-start | bytes 8192 | tf_op jit(solution)/shard_map/all_to_all | solution.py:119
  23.9 86.8 %all-to-all-start = ((bf16[4,2,32,1024]{3,2,1,0:T(8,128)(2,1)}), bf16[4,2,32,1024]{3,2,1,0:T(8,128)(2,1)S(1)}, u32[]{:S(2)}, u32[]{:S(2)}) async-start(bf16[4,2,32,1024]{3,2,1,0:T(8,128)(2,1)} %bitcast.5), calls=%async_computation | async-start | bytes 1048576 | tf_op jit(solution)/shard_map/all_to_all | solution.py:117
  110.7 18.2 %all-to-all-start.4 = ((bf16[4,2,32,1024]{3,2,1,0:T(8,128)(2,1)}), bf16[4,2,32,1024]{3,2,1,0:T(8,128)(2,1)S(1)}, u32[]{:S(2)}, u32[]{:S(2)}) async-start(bf16[4,2,32,1024]{3,2,1,0:T(8,128)(2,1)} %bitcast.20), calls=%async_computation.4 | async-start | bytes 1048576 | tf_op jit(solution)/shard_map/all_to_all | solution.py:118
  128.9 17.5 %all-to-all-start.2 = ((bf16[4,2,32,1024]{3,2,1,0:T(8,128)(2,1)}), bf16[4,2,32,1024]{3,2,1,0:T(8,128)(2,1)S(1)}, u32[]{:S(2)}, u32[]{:S(2)}) async-start(bf16[4,2,32,1024]{3,2,1,0:T(8,128)(2,1)} %bitcast.13), calls=%async_computation.2 | async-start | bytes 1048576 | tf_op jit(solution)/shard_map/all_to_all | solution.py:116
  147.4 1.0 copy-start.1
  159.5 17.4 %all-to-all-start.5 = ((bf16[4,2,32,1024]{3,2,1,0:T(8,128)(2,1)}), bf16[4,2,32,1024]{3,2,1,0:T(8,128)(2,1)S(1)}, u32[]{:S(2)}, u32[]{:S(2)}) async-start(bf16[4,2,32,1024]{3,2,1,0:T(8,128)(2,1)} %copy.100), calls=%async_computation.5 | async-start | bytes 1048576 | tf_op jit(solution)/shard_map/all_to_all | solution.py:61
  163.0 111.2 %reduce-scatter.2.cloned.1.call-start = ((), (), s32[]{:S(2)}) async-start(), calls=%async_computation.9 | async-start | bytes 5242880 | tf_op jit(solution)/shard_map/reduce_scatter | solution.py:67
  184.8 30.9 %all-to-all-start.3 = ((bf16[4,2,32,1024]{3,2,1,0:T(8,128)(2,1)}), bf16[4,2,32,1024]{3,2,1,0:T(8,128)(2,1)S(1)}, u32[]{:S(2)}, u32[]{:S(2)}) async-start(bf16[4,2,32,1024]{3,2,1,0:T(8,128)(2,1)} %copy.89), calls=%async_computation.3 | async-start | bytes 1048576 | tf_op jit(solution)/shard_map/all_to_all | solution.py:60
  215.7 60.1 %all-to-all-start.6 = ((bf16[4,2,32,1024]{3,2,1,0:T(8,128)(2,1)}), bf16[4,2,32,1024]{3,2,1,0:T(8,128)(2,1)S(1)}, u32[]{:S(2)}, u32[]{:S(2)}) async-start(bf16[4,2,32,1024]{3,2,1,0:T(8,128)(2,1)} %copy.105), calls=%async_computation.6 | async-start | bytes 1048576 | tf_op jit(solution)/shard_map/all_to_all | solution.py:62
  223.0 94.5 %all-reduce.2.cloned.1.call-start = ((), (), s32[]{:S(2)}) async-start(), calls=%async_computation.10 | async-start | bytes 2097152 | tf_op jit(solution)/shard_map/psum | solution.py:75
Sparse Core Ops, SparseCore 0:
  9.6 94.5 all-gather.1
  181.5 92.6 reduce-scatter.1
  276.7 40.7 all-reduce.1
where the time goes:
time: 328 us; the launch traced here: 327 us
  waiting for transfers between devices  224 us (68%)
  starting transfers between devices  31.3 us (10%)
  local copies, waits for them, and re-layouts  29.1 us (9%)
  matrix products  24.6 us (8%)
  between operations  14 us (4%)
  other arithmetic  3.89 us (1%)
    all_gather x1, waiting for transfers between devices, local(): weight_full = lax.all_gather(shared_weight, 'seq', axis=0, tiled=True)  74.4 us
    reduce_scatter x1, waiting for transfers between devices, weight_rows(): lax.psum_scatter(lax.dot_general(tokens, y_grad, (((0,), (0,)), ((), ()))...  51.2 us
    psum x1, waiting for transfers between devices, weight_rows(): return lax.psum(summed, 'rep').astype(jnp.float32)  35.7 us
    all_to_all x1, waiting for transfers between devices, attend_owned(): lax.all_to_all(results[0], 'seq', split_axis=0, concat_axis=0, tiled=True)  23.9 us
    all_to_all x1, waiting for transfers between devices, attend_owned(): lax.all_to_all(results[1], 'seq', split_axis=0, concat_axis=0, tiled=True)  13.7 us
    all_to_all x1, waiting for transfers between devices, local(): lax.all_to_all(place(queries), 'seq', split_axis=0, concat_axis=0, tiled=...  11.7 us
    all_to_all x1, waiting for transfers between devices, local(): lax.all_to_all(place(cotangent[0]), 'seq', split_axis=0, concat_axis=0, t...  9.11 us
    all_to_all x1, starting transfers between devices, attend_owned(): lax.all_to_all(results[2], 'seq', split_axis=0, concat_axis=0, tiled=True)  7.33 us
  transfers between devices with their start and end apart: 10, of which 8 were waited for; matrix products, arithmetic and copies ran while one was open for 12% of the time, Pallas kernels for 0%

commit v1 on v0

--- a/solution.py
+++ b/solution.py
@@ -1,6 +1,8 @@
 import jax
 import jax.numpy as jnp
 from jax import lax
+from jax.experimental import pallas as pl
+from jax.experimental.pallas import tpu as pltpu
 from jax.sharding import PartitionSpec as P
 
 HEADS = 8
@@ -130,6 +132,358 @@
     return (attended[None], hidden_grad[None], v_tok[None], weight_grad)
 
 
+SHIFTS = (1, 3, 2)
+MESH = pl.DeviceIdType.MESH
+
+
+def along_heads_kernel(
+    hidden_ref, weight_ref, values_ref, cot_ref, cid_ref,
+    att_ref, hg_ref, vg_ref, wg_ref,
+    wbuf, vbuf, gbuf, pbuf, cbuf, hbuf, ybuf, hturn, qacc, vacc, acc,
+    qbuf, sbuf_att, sbuf_vg, part, recv_core, both, recv_x,
+    wsend, wrecv, csend, crecv, vsend, vrecv, gsend, grecv, psend, precv,
+    hsend, hrecv, ysend, yrecv, asend, arecv, dsend, drecv, rsend, rrecv,
+):
+    n = 4
+    z = lax.axis_index("seq")
+    y = lax.axis_index("groups")
+    rep = lax.axis_index("rep")
+    x, core = rep // 2, rep % 2
+    tok = hidden_ref.shape[0]
+    depth = weight_ref.shape[0]
+    wide = values_ref.shape[1] // n
+    heads = wide // HEAD_SIZE
+    scale = SOFTMAX_HEAT / HEAD_SIZE
+    to_y = {"groups": 1 - y}
+    to_x = {"rep": (1 - x) * 2 + core}
+    to_core = {"rep": x * 2 + 1 - core}
+
+    def to_seq(k):
+        return {"seq": lax.rem(z + k, n)}
+
+    def source(k):
+        return lax.rem(z + n - k, n)
+
+    def span(index, size):
+        return pl.ds(pl.multiple_of(index * size, size), size)
+
+    def remote(src, dst, send, recv, device):
+        return pltpu.make_async_remote_copy(
+            src_ref=src, dst_ref=dst, send_sem=send, recv_sem=recv,
+            device_id=device, device_id_type=MESH,
+        )
+
+    barrier = pltpu.get_barrier_semaphore()
+    for peer in [to_seq(k) for k in range(1, n)] + [to_y, to_x, to_core]:
+        pl.semaphore_signal(barrier, inc=1, device_id=peer, device_id_type=MESH)
+    pl.semaphore_wait(barrier, n + 2)
+
+    started = []
+
+    def start(copy):
+        copy.start()
+        started.append(copy)
+        return copy
+
+    half = depth // 2
+    quarter = half // 2
+    eighth = quarter // 2
+    sixteenth = eighth // 2
+
+    def rows_of(stage, part_half):
+        a, b = (y, x) if part_half == 0 else (x, y)
+        base = part_half * half + core * quarter
+        if stage == 0:
+            return pl.ds(pl.multiple_of(base + b * eighth + a * sixteenth, sixteenth), sixteenth)
+        if stage == 1:
+            return pl.ds(pl.multiple_of(base + b * eighth + a * sixteenth, sixteenth), sixteenth)
+        if stage == 2:
+            return pl.ds(pl.multiple_of(base + b * eighth, eighth), eighth)
+        return pl.ds(pl.multiple_of(base, quarter), quarter)
+
+    weight_copies = {}
+
+    def weight_stage(stage, k, part_half):
+        rows = rows_of(stage, part_half)
+        if stage == 0:
+            src, device = weight_ref.at[rows], to_seq(k)
+        else:
+            src = wbuf.at[k - 1, rows]
+            first, second = (to_y, to_x) if part_half == 0 else (to_x, to_y)
+            device = (first, second, to_core)[stage - 1]
+        weight_copies[stage, k, part_half] = start(
+            remote(
+                src, wbuf.at[k - 1, rows],
+                wsend.at[stage, k - 1, part_half], wrecv.at[stage, k - 1, part_half], device,
+            )
+        )
+
+    cid_copies, v_copies, g_copies = {}, {}, {}
+    for k in SHIFTS:
+        for part_half in range(2):
+            weight_stage(0, k, part_half)
+    for k in SHIFTS:
+        peer = lax.rem(z + k, n)
+        cid_copies[k] = start(
+            remote(cid_ref, cbuf.at[z], csend.at[k - 1], crecv.at[k - 1], to_seq(k))
+        )
+        v_copies[k] = start(
+            remote(
+                values_ref.at[:, span(peer, wide)], vbuf.at[span(z, tok)],
+                vsend.at[k - 1], vrecv.at[k - 1], to_seq(k),
+            )
+        )
+        g_copies[k] = start(
+            remote(
+                cot_ref.at[:, span(peer, wide)], gbuf.at[span(z, tok)],
+                gsend.at[k - 1], grecv.at[k - 1], to_seq(k),
+            )
+        )
+    vbuf[span(z, tok), :] = values_ref[:, span(z, wide)]
+    gbuf[span(z, tok), :] = cot_ref[:, span(z, wide)]
+    cbuf[z] = cid_ref[...]
+    hbuf[span(z, tok), :] = hidden_ref[:, span(z, depth)]
+    acc[...] = jnp.dot(
+        hidden_ref[:, span(z, depth)], weight_ref[...], preferred_element_type=jnp.float32
+    )
+
+    for turn in range(len(SHIFTS) + 3):
+        for stage in range(4):
+            if 0 <= turn - stage < len(SHIFTS):
+                k = SHIFTS[turn - stage]
+                for part_half in range(2):
+                    weight_copies[stage, k, part_half].wait_recv()
+                    if stage < 3:
+                        weight_stage(stage + 1, k, part_half)
+                if stage == 3:
+                    acc[...] += jnp.dot(
+                        hidden_ref[:, span(source(k), depth)], wbuf[k - 1],
+                        preferred_element_type=jnp.float32,
+                    )
+
+    for h in range(n):
+        part[h, :tok, :] = acc[:, h * wide:(h + 1) * wide].astype(jnp.bfloat16)
+    pbuf[span(z, tok), :] = part[z, :tok, :]
+    p_copies, h_copies = {}, {}
+    for k in SHIFTS:
+        peer = lax.rem(z + k, n)
+        p_copies[k] = start(
+            remote(
+                part.at[peer, pl.ds(0, tok)], pbuf.at[span(z, tok)],
+                psend.at[k - 1], precv.at[k - 1], to_seq(k),
+            )
+        )
+    for k in SHIFTS:
+        peer = lax.rem(z + k, n)
+        h_copies[k] = start(
+            remote(
+                hidden_ref.at[:, span(peer, depth)], hbuf.at[span(z, tok)],
+                hsend.at[k - 1], hrecv.at[k - 1], to_seq(k),
+            )
+        )
+    for k in SHIFTS:
+        cid_copies[k].wait_recv()
+        v_copies[k].wait_recv()
+        g_copies[k].wait_recv()
+    for k in SHIFTS:
+        p_copies[k].wait_recv()
+        p_copies[k].wait_send()
+
+    id_rows = [cbuf[b] for b in range(n)]
+    id_cols = [jnp.transpose(block)[:, 0:1] for block in id_rows]
+    row_at = lax.broadcasted_iota(jnp.int32, (tok, tok), 0)
+    col_at = lax.broadcasted_iota(jnp.int32, (tok, tok), 1)
+    own = jnp.exp(jnp.float32(-SOFTMAX_HEAT))
+
+    y_copies, a_copies, d_copies = {}, {}, {}
+    nt = (((1,), (1,)), ((), ()))
+    tn = (((0,), (0,)), ((), ()))
+    for head in range(heads):
+        cols = pl.ds(head * HEAD_SIZE, HEAD_SIZE)
+        proj = pbuf[:, cols].astype(jnp.float32)
+        inverse = lax.rsqrt(jnp.mean(proj * proj, -1, keepdims=True) + EPSILON)
+        qbuf[head] = (proj * inverse).astype(jnp.bfloat16)
+        qacc[...] = jnp.zeros_like(qacc)
+        vacc[...] = jnp.zeros_like(vacc)
+        for b in range(n):
+            upto = (b + 1) * tok
+            rows = pl.ds(b * tok, tok)
+            q_b = qbuf[head, rows]
+            g_b = gbuf[rows, cols]
+            q_all = qbuf[head, pl.ds(0, upto)]
+            v_all = vbuf[pl.ds(0, upto), cols]
+            before = jnp.concatenate(
+                [
+                    (id_rows[j][0:1, :] == id_cols[b])
+                    & ((col_at < row_at) if j == b else (col_at >= 0))
+                    for j in range(b + 1)
+                ],
+                axis=1,
+            )
+            eye = (col_at == row_at) if b == 0 else jnp.concatenate(
+                [jnp.zeros((tok, b * tok), jnp.float32), (col_at == row_at).astype(jnp.float32)],
+                axis=1,
+            ) > 0.5
+            scores = lax.dot_general(q_b, q_all, nt, preferred_element_type=jnp.float32) * scale
+            terms = jnp.where(
+                before, jnp.exp(scores - SOFTMAX_HEAT), jnp.where(eye, own, 0.0)
+            )
+            probs = terms * (1.0 / jnp.sum(terms, -1, keepdims=True))
+            low = probs.astype(jnp.bfloat16)
+            sbuf_att[head, rows] = jnp.dot(
+                low, v_all, preferred_element_type=jnp.float32
+            ).astype(jnp.bfloat16)
+            dprob = lax.dot_general(g_b, v_all, nt, preferred_element_type=jnp.float32)
+            delta = jnp.sum(probs * dprob, -1, keepdims=True)
+            dscore = jnp.where(before, probs * (dprob - delta), 0.0).astype(jnp.bfloat16)
+            qacc[rows, :] += jnp.dot(dscore, q_all, preferred_element_type=jnp.float32)
+            qacc[pl.ds(0, upto), :] += lax.dot_general(
+                dscore, q_b, tn, preferred_element_type=jnp.float32
+            )
+            vacc[pl.ds(0, upto), :] += lax.dot_general(
+                low, g_b, tn, preferred_element_type=jnp.float32
+            )
+        dq = (qacc[...] * scale).astype(jnp.bfloat16).astype(jnp.float32)
+        dy = inverse * dq - proj * inverse**3 * jnp.mean(dq * proj, -1, keepdims=True)
+        ybuf[0, :, cols] = dy.astype(jnp.bfloat16)
+        sbuf_vg[head] = vacc[...].astype(jnp.bfloat16)
+        for k in SHIFTS:
+            y_copies[k, head] = start(
+                remote(
+                    ybuf.at[0, :, cols], ybuf.at[k, :, cols],
+                    ysend.at[k - 1, head], yrecv.at[k - 1, head], to_seq(k),
+                )
+            )
+        place = pl.ds(pl.multiple_of(z * wide + head * HEAD_SIZE, HEAD_SIZE), HEAD_SIZE)
+        for k in SHIFTS:
+            peer = lax.rem(z + k, n)
+            a_copies[k, head] = start(
+                remote(
+                    sbuf_att.at[head, span(peer, tok)], att_ref.at[:, place],
+                    asend.at[k - 1, head], arecv.at[k - 1, head], to_seq(k),
+                )
+            )
+            d_copies[k, head] = start(
+                remote(
+                    sbuf_vg.at[head, span(peer, tok)], vg_ref.at[:, place],
+                    dsend.at[k - 1, head], drecv.at[k - 1, head], to_seq(k),
+                )
+            )
+        att_ref[:, place] = sbuf_att[head, span(z, tok)]
+        vg_ref[:, place] = sbuf_vg[head, span(z, tok)]
+
+    for k in SHIFTS:
+        h_copies[k].wait_recv()
+    hturn[...] = jnp.transpose(hbuf[...])
+
+    mid = depth // 2
+    mine = pl.ds(pl.multiple_of(core * mid, mid), mid)
+    other = pl.ds(pl.multiple_of((1 - core) * mid, mid), mid)
+    core_copies, x_copies, last_copies = {}, {}, {}
+
+    def add_chips(k):
+        x_copies[k].wait_recv()
+        at = span(source(k), wide)
+        total = both[k].astype(jnp.float32) + recv_x[k].astype(jnp.float32)
+        wg_ref[mine, at] = total.astype(jnp.bfloat16)
+        last_copies[k] = start(
+            remote(
+                wg_ref.at[mine, at], wg_ref.at[mine, at],
+                rsend.at[2, k], rrecv.at[2, k], to_core,
+            )
+        )
+
+    order = (0,) + SHIFTS
+    for step, k in enumerate(order):
+        if k > 0:
+            for head in range(heads):
+                y_copies[k, head].wait_recv()
+        part[k] = jnp.dot(hturn[...], ybuf[k], preferred_element_type=jnp.float32).astype(
+            jnp.bfloat16
+        )
+        core_copies[k] = start(
+            remote(part.at[k, other], recv_core.at[k], rsend.at[0, k], rrecv.at[0, k], to_core)
+        )
+        if step >= 1:
+            add_chips(order[step - 1])
+        core_copies[k].wait_recv()
+        both[k] = (
+            part[k, mine, :].astype(jnp.float32) + recv_core[k].astype(jnp.float32)
+        ).astype(jnp.bfloat16)
+        x_copies[k] = start(
+            remote(both.at[k], recv_x.at[k], rsend.at[1, k], rrecv.at[1, k], to_x)
+        )
+
+    own_rows = span(z, tok)
+    for k in range(n):
+        block = weight_ref if k == 0 else wbuf.at[k - 1]
+        total = jnp.zeros((tok, depth), jnp.float32)
+        for j in range(n):
+            h = source(j)
+            total = total + lax.dot_general(
+                ybuf[j, own_rows, :], block[:, span(h, wide)], nt,
+                preferred_element_type=jnp.float32,
+            )
+        hg_ref[:, span(source(k), depth)] = total.astype(jnp.bfloat16)
+    add_chips(order[-1])
+
+    for k in SHIFTS:
+        for head in range(heads):
+            a_copies[k, head].wait_recv()
+            d_copies[k, head].wait_recv()
+    for k in order:
+        last_copies[k].wait_recv()
+    done = set(id(copy) for copy in p_copies.values())
+    for copy in started:
+        if id(copy) not in done:
+            copy.wait_send()
+
+
+def local_by_heads(hidden, shared_weight, values, clusters, cotangent):
+    n = 4
+    tok, model = hidden.shape[1:]
+    depth, width = shared_weight.shape
+    wide = width // n
+    length = n * tok
+    heads = wide // HEAD_SIZE
+    ids = jnp.broadcast_to(clusters[0, :, 0].astype(jnp.float32)[None, :], (8, tok))
+    bf, f32 = jnp.bfloat16, jnp.float32
+    vm = pltpu.VMEM
+    dma = pltpu.SemaphoreType.DMA
+    scratch = [
+        vm((n - 1, depth, width), bf), vm((length, wide), bf), vm((length, wide), bf),
+        vm((length, wide), bf), vm((n, 8, tok), f32), vm((length, depth), bf),
+        vm((n, length, wide), bf), vm((depth, length), bf), vm((length, HEAD_SIZE), f32),
+        vm((length, HEAD_SIZE), f32), vm((tok, width), f32),
+        vm((heads, length, HEAD_SIZE), bf), vm((heads, length, HEAD_SIZE), bf),
+        vm((heads, length, HEAD_SIZE), bf), vm((n, depth, wide), bf),
+        vm((n, depth // 2, wide), bf), vm((n, depth // 2, wide), bf), vm((n, depth // 2, wide), bf),
+        dma((4, n - 1, 2)), dma((4, n - 1, 2)),
+    ]
+    scratch += [dma((n - 1,)) for _ in range(10)]
+    scratch += [dma((n - 1, heads)) for _ in range(6)]
+    scratch += [dma((3, n)), dma((3, n))]
+    att, hg, vg, wg = pl.pallas_call(
+        along_heads_kernel,
+        out_shape=(
+            jax.ShapeDtypeStruct((tok, width), bf),
+            jax.ShapeDtypeStruct((tok, model), bf),
+            jax.ShapeDtypeStruct((tok, width), bf),
+            jax.ShapeDtypeStruct((depth, width), bf),
+        ),
+        in_specs=[pl.BlockSpec(memory_space=pltpu.VMEM)] * 5,
+        out_specs=[pl.BlockSpec(memory_space=pltpu.VMEM)] * 4,
+        scratch_shapes=scratch,
+        compiler_params=pltpu.CompilerParams(
+            collective_id=0, has_side_effects=True, vmem_limit_bytes=48 * 1024 * 1024
+        ),
+        cost_estimate=pl.CostEstimate(
+            flops=8 * tok * model * width, bytes_accessed=8 * 1024 * 1024, transcendentals=length * length
+        ),
+    )(hidden[0], shared_weight, values[0], cotangent[0], ids)
+    return att[None], hg[None], vg[None], wg.astype(f32)
+
+
 def solution(mesh):
     placed = (
         P(("groups", "rep"), "seq", None),
@@ -138,8 +492,9 @@
         P(("groups", "rep"), "seq", None),
         P(("groups", "rep"), "seq", None),
     )
+    by_heads = (mesh.shape["groups"], mesh.shape["seq"], mesh.shape["rep"]) == (2, 4, 4)
     return jax.shard_map(
-        local,
+        local_by_heads if by_heads else local,
         mesh=mesh,
         in_specs=placed,
         out_specs=(

time: 328 us -> 99.8 us (0.30)
  the two profiles are of different devices: /device:TPU:0 before, /device:TPU:21 now
where the time goes in v1:
time: 99.8 us; the launch traced here: 99.6 us
  Pallas kernels  90.3 us (90%)
  local copies, waits for them, and re-layouts  6.37 us (6%)
  other arithmetic  2.24 us (2%)
    pallas_call x1, Pallas kernels, local_by_heads(): pl.pallas_call(along_heads_kernel, out_shape=(jax.ShapeDtypeStruct((tok,...  90.3 us
    unnamed x11, local copies, waits for them, and re-layouts  6.36 us

profile of v1, /device:TPU:21, one launch (start us, length us, event | category | flops | bytes accessed | tf_op | source)
XLA Modules:
  0.0 99.6 jit_solution(2095630879050715593)
XLA Ops:
  0.6 0.7 convert_bitcast_fusion
  1.3 0.0 copy-start
  1.3 1.2 %copy-done = bf16[512,1024]{1,0:T(8,128)(2,1)S(1)} copy-done((bf16[512,1024]{1,0:T(8,128)(2,1)S(1)}, bf16[512,1024]{1,0:T(8,128)(2,1)}, u32[]{:S(2)}) %copy-start) | copy-done | bytes 1048600
  2.5 0.0 copy-start.1
  2.5 1.0 %copy-done.1 = bf16[1,128,2048]{2,1,0:T(8,128)(2,1)S(1)} copy-done((bf16[1,128,2048]{2,1,0:T(8,128)(2,1)S(1)}, bf16[1,128,2048]{2,1,0:T(8,128)(2,1)}, u32[]{:S(2)}) %copy-start.1) | copy-done | bytes 524312
  3.6 0.0 copy-start.2
  3.6 0.9 copy-done.2
  4.5 0.0 copy-start.3
  4.5 0.9 copy-done.3
  5.5 90.3 %shard_map.84 = (bf16[128,1024]{1,0:T(8,128)(2,1)S(1)}, bf16[128,2048]{1,0:T(8,128)(2,1)S(1)}, bf16[128,1024]{1,0:T(8,128)(2,1)S(1)}, bf16[512,1024]{1,0:T(8,128)(2,1)S(1)}) custom-call(bf16[128,2048]{1,0:T(8,128)(2,1)S(1)} %bitcast.11, bf16[512,1024]{1,0:T(8,128)(2,1)S(1)} %copy-done, bf16[128,1024]{1,0:T(8,128)(2,1)S(1)} %bitcast.12, ...), custom_call_target="tpu_custom_call" | custom-call | flops 2147483648 | bytes 8388608 | tf_op jit(solution)/shard_map/pallas_call | solution.py:466
  95.8 1.6 %convert_element_type.15 = f32[512,1024]{1,0:T(8,128)} convert(bf16[512,1024]{1,0:T(8,128)(2,1)S(1)} %get-tuple-element.11) | non-fusion elementwise | flops 524288 | bytes 3145728 | tf_op jit(solution)/shard_map/convert_element_type | solution.py:484
  97.4 0.7 copy.12
  98.1 0.8 copy.13
  98.9 0.7 copy.14
  (1 shorter events, 0.0 us)
Async XLA Ops:
  1.3 1.2 %copy-start = (bf16[512,1024]{1,0:T(8,128)(2,1)S(1)}, bf16[512,1024]{1,0:T(8,128)(2,1)}, u32[]{:S(2)}) copy-start(bf16[512,1024]{1,0:T(8,128)(2,1)} %weight_ref.1) | copy-start | bytes 3145732
  2.5 1.0 %copy-start.1 = (bf16[1,128,2048]{2,1,0:T(8,128)(2,1)S(1)}, bf16[1,128,2048]{2,1,0:T(8,128)(2,1)}, u32[]{:S(2)}) copy-start(bf16[1,128,2048]{2,1,0:T(8,128)(2,1)} %param.5) | copy-start | bytes 1572868
  3.6 0.9 copy-start.2
  4.5 0.9 copy-start.3

commit v2 on v1

--- a/solution.py
+++ b/solution.py
@@ -137,11 +137,11 @@
 
 
 def along_heads_kernel(
-    hidden_ref, weight_ref, values_ref, cot_ref, cid_ref,
+    hidden_hbm, weight_hbm, values_hbm, cot_hbm, cid_ref,
     att_ref, hg_ref, vg_ref, wg_ref,
-    wbuf, vbuf, gbuf, pbuf, cbuf, hbuf, ybuf, hturn, qacc, vacc, acc,
+    hidden_ref, wbuf, vbuf, gbuf, pbuf, cbuf, hbuf, ybuf, hturn, qacc, vacc, acc,
     qbuf, sbuf_att, sbuf_vg, part, recv_core, both, recv_x,
-    wsend, wrecv, csend, crecv, vsend, vrecv, gsend, grecv, psend, precv,
+    local_sem, zsend, zrecv, wsend, wrecv, csend, crecv, vsend, vrecv, gsend, grecv, psend, precv,
     hsend, hrecv, ysend, yrecv, asend, arecv, dsend, drecv, rsend, rrecv,
 ):
     n = 4
@@ -150,8 +150,8 @@
     rep = lax.axis_index("rep")
     x, core = rep // 2, rep % 2
     tok = hidden_ref.shape[0]
-    depth = weight_ref.shape[0]
-    wide = values_ref.shape[1] // n
+    depth = weight_hbm.shape[0]
+    wide = values_hbm.shape[1] // n
     heads = wide // HEAD_SIZE
     scale = SOFTMAX_HEAT / HEAD_SIZE
     to_y = {"groups": 1 - y}
@@ -161,8 +161,10 @@
     def to_seq(k):
         return {"seq": lax.rem(z + k, n)}
 
-    def source(k):
-        return lax.rem(z + n - k, n)
+    inner = (z * (n - 1 - z)) > 0
+    outward = {"seq": z + 1 - 2 * (z % 2)}
+    across = {"seq": n - 1 - z}
+    origins = (z, z + 1 - 2 * (z % 2), 2 - z // 2, 3 - 3 * (z // 2))
 
     def span(index, size):
         return pl.ds(pl.multiple_of(index * size, size), size)
@@ -173,17 +175,45 @@
             device_id=device, device_id_type=MESH,
         )
 
+    loads = [
+        pltpu.make_async_copy(src, dst, local_sem.at[index])
+        for index, (src, dst) in enumerate(
+            [
+                (hidden_hbm, hidden_ref),
+                (weight_hbm, wbuf.at[z]),
+                (values_hbm.at[:, span(z, wide)], vbuf.at[span(z, tok)]),
+                (cot_hbm.at[:, span(z, wide)], gbuf.at[span(z, tok)]),
+                (hidden_hbm.at[:, span(z, depth)], hbuf.at[span(z, tok)]),
+            ]
+        )
+    ]
+    for load in loads:
+        load.start()
+
     barrier = pltpu.get_barrier_semaphore()
     for peer in [to_seq(k) for k in range(1, n)] + [to_y, to_x, to_core]:
         pl.semaphore_signal(barrier, inc=1, device_id=peer, device_id_type=MESH)
     pl.semaphore_wait(barrier, n + 2)
 
-    started = []
+    started, relayed = [], []
 
     def start(copy):
         copy.start()
         started.append(copy)
         return copy
+
+    def relay(step, src, dst, send, recv):
+        if step == 0:
+            start(remote(src, dst, send.at[0], recv, outward))
+        to_middle = step < 2
+        copy = remote(
+            src, dst, send.at[1 + step], recv, across if to_middle else outward
+        )
+        relayed.append(copy)
+
+        @pl.when(inner)
+        def _():
+            copy.start()
 
     half = depth // 2
     quarter = half // 2
@@ -203,25 +233,29 @@
 
     weight_copies = {}
 
-    def weight_stage(stage, k, part_half):
+    def weight_relay(step, part_half):
+        rows = rows_of(0, part_half)
+        block = wbuf.at[origins[step], rows]
+        relay(
+            step, weight_hbm.at[rows] if step == 0 else block, block,
+            zsend.at[part_half], zrecv.at[origins[step], part_half],
+        )
+
+    def weight_stage(stage, step, part_half):
         rows = rows_of(stage, part_half)
-        if stage == 0:
-            src, device = weight_ref.at[rows], to_seq(k)
-        else:
-            src = wbuf.at[k - 1, rows]
-            first, second = (to_y, to_x) if part_half == 0 else (to_x, to_y)
-            device = (first, second, to_core)[stage - 1]
-        weight_copies[stage, k, part_half] = start(
-            remote(
-                src, wbuf.at[k - 1, rows],
-                wsend.at[stage, k - 1, part_half], wrecv.at[stage, k - 1, part_half], device,
+        block = wbuf.at[origins[step], rows]
+        first, second = (to_y, to_x) if part_half == 0 else (to_x, to_y)
+        weight_copies[stage, step, part_half] = start(
+            remote(
+                block, block,
+                wsend.at[stage - 1, step - 1, part_half], wrecv.at[stage - 1, step - 1, part_half],
+                (first, second, to_core)[stage - 1],
             )
         )
 
     cid_copies, v_copies, g_copies = {}, {}, {}
-    for k in SHIFTS:
-        for part_half in range(2):
-            weight_stage(0, k, part_half)
+    for part_half in range(2):
+        weight_relay(0, part_half)
     for k in SHIFTS:
         peer = lax.rem(z + k, n)
         cid_copies[k] = start(
@@ -229,35 +263,42 @@
         )
         v_copies[k] = start(
             remote(
-                values_ref.at[:, span(peer, wide)], vbuf.at[span(z, tok)],
+                values_hbm.at[:, span(peer, wide)], vbuf.at[span(z, tok)],
                 vsend.at[k - 1], vrecv.at[k - 1], to_seq(k),
             )
         )
         g_copies[k] = start(
             remote(
-                cot_ref.at[:, span(peer, wide)], gbuf.at[span(z, tok)],
+                cot_hbm.at[:, span(peer, wide)], gbuf.at[span(z, tok)],
                 gsend.at[k - 1], grecv.at[k - 1], to_seq(k),
             )
         )
-    vbuf[span(z, tok), :] = values_ref[:, span(z, wide)]
-    gbuf[span(z, tok), :] = cot_ref[:, span(z, wide)]
     cbuf[z] = cid_ref[...]
-    hbuf[span(z, tok), :] = hidden_ref[:, span(z, depth)]
+    for load in loads:
+        load.wait()
     acc[...] = jnp.dot(
-        hidden_ref[:, span(z, depth)], weight_ref[...], preferred_element_type=jnp.float32
-    )
-
-    for turn in range(len(SHIFTS) + 3):
-        for stage in range(4):
-            if 0 <= turn - stage < len(SHIFTS):
-                k = SHIFTS[turn - stage]
+        hidden_ref[:, span(z, depth)], wbuf[z], preferred_element_type=jnp.float32
+    )
+
+    for turn in range(n + 2):
+        for stage in range(n):
+            step = turn - stage + 1
+            if 1 <= step < n:
                 for part_half in range(2):
-                    weight_copies[stage, k, part_half].wait_recv()
+                    if stage == 0:
+                        block = wbuf.at[origins[step], rows_of(0, part_half)]
+                        remote(
+                            block, block, zsend.at[part_half, 0],
+                            zrecv.at[origins[step], part_half], outward,
+                        ).wait_recv()
+                        weight_relay(step, part_half)
+                    else:
+                        weight_copies[stage, step, part_half].wait_recv()
                     if stage < 3:
-                        weight_stage(stage + 1, k, part_half)
+                        weight_stage(stage + 1, step, part_half)
                 if stage == 3:
                     acc[...] += jnp.dot(
-                        hidden_ref[:, span(source(k), depth)], wbuf[k - 1],
+                        hidden_ref[:, span(origins[step], depth)], wbuf[origins[step]],
                         preferred_element_type=jnp.float32,
                     )
 
@@ -277,7 +318,7 @@
         peer = lax.rem(z + k, n)
         h_copies[k] = start(
             remote(
-                hidden_ref.at[:, span(peer, depth)], hbuf.at[span(z, tok)],
+                hidden_hbm.at[:, span(peer, depth)], hbuf.at[span(z, tok)],
                 hsend.at[k - 1], hrecv.at[k - 1], to_seq(k),
             )
         )
@@ -295,7 +336,34 @@
     col_at = lax.broadcasted_iota(jnp.int32, (tok, tok), 1)
     own = jnp.exp(jnp.float32(-SOFTMAX_HEAT))
 
-    y_copies, a_copies, d_copies = {}, {}, {}
+    a_copies, d_copies = {}, {}
+
+    def y_relay(step, head):
+        block = ybuf.at[origins[step], :, pl.ds(head * HEAD_SIZE, HEAD_SIZE)]
+        if step > 0:
+            remote(
+                block, block, ysend.at[head, 0], yrecv.at[origins[step], head], outward
+            ).wait_recv()
+        relay(step, block, block, ysend.at[head], yrecv.at[origins[step], head])
+
+    def send_back():
+        for head in range(heads):
+            place = pl.ds(pl.multiple_of(z * wide + head * HEAD_SIZE, HEAD_SIZE), HEAD_SIZE)
+            for k in SHIFTS:
+                peer = lax.rem(z + k, n)
+                a_copies[k, head] = start(
+                    remote(
+                        sbuf_att.at[head, span(peer, tok)], att_ref.at[:, place],
+                        asend.at[k - 1, head], arecv.at[k - 1, head], to_seq(k),
+                    )
+                )
+                d_copies[k, head] = start(
+                    remote(
+                        sbuf_vg.at[head, span(peer, tok)], vg_ref.at[:, place],
+                        dsend.at[k - 1, head], drecv.at[k - 1, head], to_seq(k),
+                    )
+                )
+
     nt = (((1,), (1,)), ((), ()))
     tn = (((0,), (0,)), ((), ()))
     for head in range(heads):
@@ -345,30 +413,10 @@
             )
         dq = (qacc[...] * scale).astype(jnp.bfloat16).astype(jnp.float32)
         dy = inverse * dq - proj * inverse**3 * jnp.mean(dq * proj, -1, keepdims=True)
-        ybuf[0, :, cols] = dy.astype(jnp.bfloat16)
+        ybuf[z, :, cols] = dy.astype(jnp.bfloat16)
         sbuf_vg[head] = vacc[...].astype(jnp.bfloat16)
-        for k in SHIFTS:
-            y_copies[k, head] = start(
-                remote(
-                    ybuf.at[0, :, cols], ybuf.at[k, :, cols],
-                    ysend.at[k - 1, head], yrecv.at[k - 1, head], to_seq(k),
-                )
-            )
+        y_relay(0, head)
         place = pl.ds(pl.multiple_of(z * wide + head * HEAD_SIZE, HEAD_SIZE), HEAD_SIZE)
-        for k in SHIFTS:
-            peer = lax.rem(z + k, n)
-            a_copies[k, head] = start(
-                remote(
-                    sbuf_att.at[head, span(peer, tok)], att_ref.at[:, place],
-                    asend.at[k - 1, head], arecv.at[k - 1, head], to_seq(k),
-                )
-            )
-            d_copies[k, head] = start(
-                remote(
-                    sbuf_vg.at[head, span(peer, tok)], vg_ref.at[:, place],
-                    dsend.at[k - 1, head], drecv.at[k - 1, head], to_seq(k),
-                )
-            )
         att_ref[:, place] = sbuf_att[head, span(z, tok)]
         vg_ref[:, place] = sbuf_vg[head, span(z, tok)]
 
@@ -383,7 +431,7 @@
 
     def add_chips(k):
         x_copies[k].wait_recv()
-        at = span(source(k), wide)
+        at = span(origins[k], wide)
         total = both[k].astype(jnp.float32) + recv_x[k].astype(jnp.float32)
         wg_ref[mine, at] = total.astype(jnp.bfloat16)
         last_copies[k] = start(
@@ -393,19 +441,20 @@
             )
         )
 
-    order = (0,) + SHIFTS
-    for step, k in enumerate(order):
+    for k in range(n):
         if k > 0:
             for head in range(heads):
-                y_copies[k, head].wait_recv()
-        part[k] = jnp.dot(hturn[...], ybuf[k], preferred_element_type=jnp.float32).astype(
-            jnp.bfloat16
-        )
+                y_relay(k, head)
+        if k == 2:
+            send_back()
+        part[k] = jnp.dot(
+            hturn[...], ybuf[origins[k]], preferred_element_type=jnp.float32
+        ).astype(jnp.bfloat16)
         core_copies[k] = start(
             remote(part.at[k, other], recv_core.at[k], rsend.at[0, k], rrecv.at[0, k], to_core)
         )
-        if step >= 1:
-            add_chips(order[step - 1])
+        if k > 0:
+            add_chips(k - 1)
         core_copies[k].wait_recv()
         both[k] = (
             part[k, mine, :].astype(jnp.float32) + recv_core[k].astype(jnp.float32)
@@ -416,26 +465,29 @@
 
     own_rows = span(z, tok)
     for k in range(n):
-        block = weight_ref if k == 0 else wbuf.at[k - 1]
         total = jnp.zeros((tok, depth), jnp.float32)
         for j in range(n):
-            h = source(j)
             total = total + lax.dot_general(
-                ybuf[j, own_rows, :], block[:, span(h, wide)], nt,
+                ybuf[origins[j], own_rows, :], wbuf[origins[k], :, span(origins[j], wide)], nt,
                 preferred_element_type=jnp.float32,
             )
-        hg_ref[:, span(source(k), depth)] = total.astype(jnp.bfloat16)
-    add_chips(order[-1])
+        hg_ref[:, span(origins[k], depth)] = total.astype(jnp.bfloat16)
+    add_chips(n - 1)
 
     for k in SHIFTS:
         for head in range(heads):
             a_copies[k, head].wait_recv()
             d_copies[k, head].wait_recv()
-    for k in order:
+    for k in range(n):
         last_copies[k].wait_recv()
     done = set(id(copy) for copy in p_copies.values())
     for copy in started:
         if id(copy) not in done:
+            copy.wait_send()
+
+    @pl.when(inner)
+    def _():
+        for copy in relayed:
             copy.wait_send()
 
 
@@ -451,17 +503,18 @@
     vm = pltpu.VMEM
     dma = pltpu.SemaphoreType.DMA
     scratch = [
-        vm((n - 1, depth, width), bf), vm((length, wide), bf), vm((length, wide), bf),
+        vm((tok, model), bf), vm((n, depth, width), bf), vm((length, wide), bf), vm((length, wide), bf),
         vm((length, wide), bf), vm((n, 8, tok), f32), vm((length, depth), bf),
         vm((n, length, wide), bf), vm((depth, length), bf), vm((length, HEAD_SIZE), f32),
         vm((length, HEAD_SIZE), f32), vm((tok, width), f32),
         vm((heads, length, HEAD_SIZE), bf), vm((heads, length, HEAD_SIZE), bf),
         vm((heads, length, HEAD_SIZE), bf), vm((n, depth, wide), bf),
         vm((n, depth // 2, wide), bf), vm((n, depth // 2, wide), bf), vm((n, depth // 2, wide), bf),
-        dma((4, n - 1, 2)), dma((4, n - 1, 2)),
+        dma((5,)), dma((2, n + 1)), dma((n, 2)), dma((3, n - 1, 2)), dma((3, n - 1, 2)),
     ]
     scratch += [dma((n - 1,)) for _ in range(10)]
-    scratch += [dma((n - 1, heads)) for _ in range(6)]
+    scratch += [dma((heads, n + 1)), dma((n, heads))]
+    scratch += [dma((n - 1, heads)) for _ in range(4)]
     scratch += [dma((3, n)), dma((3, n))]
     att, hg, vg, wg = pl.pallas_call(
         along_heads_kernel,
@@ -471,7 +524,8 @@
             jax.ShapeDtypeStruct((tok, width), bf),
             jax.ShapeDtypeStruct((depth, width), bf),
         ),
-        in_specs=[pl.BlockSpec(memory_space=pltpu.VMEM)] * 5,
+        in_specs=[pl.BlockSpec(memory_space=pl.ANY)] * 4
+        + [pl.BlockSpec(memory_space=pltpu.VMEM)],
         out_specs=[pl.BlockSpec(memory_space=pltpu.VMEM)] * 4,
         scratch_shapes=scratch,
         compiler_params=pltpu.CompilerParams(

time: 99.8 us -> 96.4 us (0.966)
  the two profiles are of different devices: /device:TPU:21 before, /device:TPU:0 now
where the time goes in v2:
time: 96.4 us; the launch traced here: 96.2 us
  Pallas kernels  86.9 us (90%)
  local copies, waits for them, and re-layouts  6.37 us (7%)
  other arithmetic  2.24 us (2%)
    pallas_call x1, Pallas kernels, local_by_heads(): pl.pallas_call(along_heads_kernel, out_shape=(jax.ShapeDtypeStruct((tok,...  86.9 us
    unnamed x11, local copies, waits for them, and re-layouts  6.36 us

profile of v2, /device:TPU:0, one launch (start us, length us, event | category | flops | bytes accessed | tf_op | source)
XLA Modules:
  0.0 96.2 jit_solution(11916994283837552007)
XLA Ops:
  0.6 0.7 convert_bitcast_fusion
  1.3 0.0 copy-start
  1.3 1.2 %copy-done = bf16[512,1024]{1,0:T(8,128)(2,1)S(1)} copy-done((bf16[512,1024]{1,0:T(8,128)(2,1)S(1)}, bf16[512,1024]{1,0:T(8,128)(2,1)}, u32[]{:S(2)}) %copy-start) | copy-done | bytes 1048600
  2.5 0.0 copy-start.1
  2.5 1.0 %copy-done.1 = bf16[1,128,2048]{2,1,0:T(8,128)(2,1)S(1)} copy-done((bf16[1,128,2048]{2,1,0:T(8,128)(2,1)S(1)}, bf16[1,128,2048]{2,1,0:T(8,128)(2,1)}, u32[]{:S(2)}) %copy-start.1) | copy-done | bytes 524312
  3.6 0.0 copy-start.2
  3.6 0.9 copy-done.2
  4.5 0.0 copy-start.3
  4.5 0.9 copy-done.3
  5.5 86.9 %shard_map.84 = (bf16[128,1024]{1,0:T(8,128)(2,1)S(1)}, bf16[128,2048]{1,0:T(8,128)(2,1)S(1)}, bf16[128,1024]{1,0:T(8,128)(2,1)S(1)}, bf16[512,1024]{1,0:T(8,128)(2,1)S(1)}) custom-call(bf16[128,2048]{1,0:T(8,128)(2,1)S(1)} %bitcast.11, bf16[512,1024]{1,0:T(8,128)(2,1)S(1)} %copy-done, bf16[128,1024]{1,0:T(8,128)(2,1)S(1)} %bitcast.12, ...), custom_call_target="tpu_custom_call" | custom-call | flops 2147483648 | bytes 8388608 | tf_op jit(solution)/shard_map/pallas_call | solution.py:519
  92.4 1.6 %convert_element_type.15 = f32[512,1024]{1,0:T(8,128)} convert(bf16[512,1024]{1,0:T(8,128)(2,1)S(1)} %get-tuple-element.11) | non-fusion elementwise | flops 524288 | bytes 3145728 | tf_op jit(solution)/shard_map/convert_element_type | solution.py:538
  94.0 0.7 copy.12
  94.7 0.8 copy.13
  95.4 0.7 copy.14
  (1 shorter events, 0.0 us)
Async XLA Ops:
  1.3 1.2 %copy-start = (bf16[512,1024]{1,0:T(8,128)(2,1)S(1)}, bf16[512,1024]{1,0:T(8,128)(2,1)}, u32[]{:S(2)}) copy-start(bf16[512,1024]{1,0:T(8,128)(2,1)} %weight_hbm.1) | copy-start | bytes 3145732
  2.5 1.0 %copy-start.1 = (bf16[1,128,2048]{2,1,0:T(8,128)(2,1)S(1)}, bf16[1,128,2048]{2,1,0:T(8,128)(2,1)}, u32[]{:S(2)}) copy-start(bf16[1,128,2048]{2,1,0:T(8,128)(2,1)} %param.5) | copy-start | bytes 1572868
  3.6 0.9 copy-start.2
  4.5 0.9 copy-start.3

commit v3 on v2

--- a/solution.py
+++ b/solution.py
@@ -261,18 +261,20 @@
         cid_copies[k] = start(
             remote(cid_ref, cbuf.at[z], csend.at[k - 1], crecv.at[k - 1], to_seq(k))
         )
-        v_copies[k] = start(
+
+    def send_rows(kind, k):
+        peer = lax.rem(z + k, n)
+        src, dst, send, recv, kept = (
+            (values_hbm, vbuf, vsend, vrecv, v_copies), (cot_hbm, gbuf, gsend, grecv, g_copies)
+        )[kind]
+        kept[k] = start(
             remote(
-                values_hbm.at[:, span(peer, wide)], vbuf.at[span(z, tok)],
-                vsend.at[k - 1], vrecv.at[k - 1], to_seq(k),
-            )
-        )
-        g_copies[k] = start(
-            remote(
-                cot_hbm.at[:, span(peer, wide)], gbuf.at[span(z, tok)],
-                gsend.at[k - 1], grecv.at[k - 1], to_seq(k),
-            )
-        )
+                src.at[:, span(peer, wide)], dst.at[span(z, tok)],
+                send.at[k - 1], recv.at[k - 1], to_seq(k),
+            )
+        )
+
+    waiting = [(kind, k) for kind in range(2) for k in SHIFTS]
     cbuf[z] = cid_ref[...]
     for load in loads:
         load.wait()
@@ -301,6 +303,9 @@
                         hidden_ref[:, span(origins[step], depth)], wbuf[origins[step]],
                         preferred_element_type=jnp.float32,
                     )
+        if turn >= 2:
+            for kind, k in waiting[2 * (turn - 2):2 * (turn - 1)]:
+                send_rows(kind, k)
 
     for h in range(n):
         part[h, :tok, :] = acc[:, h * wide:(h + 1) * wide].astype(jnp.bfloat16)
@@ -346,21 +351,19 @@
             ).wait_recv()
         relay(step, block, block, ysend.at[head], yrecv.at[origins[step], head])
 
-    def send_back():
+    def send_back(which):
         for head in range(heads):
             place = pl.ds(pl.multiple_of(z * wide + head * HEAD_SIZE, HEAD_SIZE), HEAD_SIZE)
             for k in SHIFTS:
                 peer = lax.rem(z + k, n)
-                a_copies[k, head] = start(
+                src, dst, send, recv, kept = (
+                    (sbuf_att, att_ref, asend, arecv, a_copies),
+                    (sbuf_vg, vg_ref, dsend, drecv, d_copies),
+                )[which]
+                kept[k, head] = start(
                     remote(
-                        sbuf_att.at[head, span(peer, tok)], att_ref.at[:, place],
-                        asend.at[k - 1, head], arecv.at[k - 1, head], to_seq(k),
-                    )
-                )
-                d_copies[k, head] = start(
-                    remote(
-                        sbuf_vg.at[head, span(peer, tok)], vg_ref.at[:, place],
-                        dsend.at[k - 1, head], drecv.at[k - 1, head], to_seq(k),
+                        src.at[head, span(peer, tok)], dst.at[:, place],
+                        send.at[k - 1, head], recv.at[k - 1, head], to_seq(k),
                     )
                 )
 
@@ -446,7 +449,7 @@
             for head in range(heads):
                 y_relay(k, head)
         if k == 2:
-            send_back()
+            send_back(0)
         part[k] = jnp.dot(
             hturn[...], ybuf[origins[k]], preferred_element_type=jnp.float32
         ).astype(jnp.bfloat16)
@@ -463,6 +466,7 @@
             remote(both.at[k], recv_x.at[k], rsend.at[1, k], rrecv.at[1, k], to_x)
         )
 
+    send_back(1)
     own_rows = span(z, tok)
     for k in range(n):
         total = jnp.zeros((tok, depth), jnp.float32)

time: 96.4 us -> 90.6 us (0.940)
  Pallas kernels: 86.9 us -> 80.4 us
    pallas_call x1, Pallas kernels: 86.9 us -> 80.4 us  [local_by_heads(): pl.pallas_call(along_heads_kernel, out_shape=(jax.ShapeDtypeStruct((tok,...]
where the time goes in v3:
time: 90.6 us; the launch traced here: 89.7 us
  Pallas kernels  80.4 us (89%)
  local copies, waits for them, and re-layouts  6.37 us (7%)
  other arithmetic  2.24 us (2%)
    pallas_call x1, Pallas kernels, local_by_heads(): pl.pallas_call(along_heads_kernel, out_shape=(jax.ShapeDtypeStruct((tok,...  80.4 us
    unnamed x11, local copies, waits for them, and re-layouts  6.36 us

profile of v3, /device:TPU:0, one launch (start us, length us, event | category | flops | bytes accessed | tf_op | source)
XLA Modules:
  0.0 89.7 jit_solution(1330722743777359956)
XLA Ops:
  0.6 0.7 convert_bitcast_fusion
  1.3 0.0 copy-start
  1.3 1.2 %copy-done = bf16[512,1024]{1,0:T(8,128)(2,1)S(1)} copy-done((bf16[512,1024]{1,0:T(8,128)(2,1)S(1)}, bf16[512,1024]{1,0:T(8,128)(2,1)}, u32[]{:S(2)}) %copy-start) | copy-done | bytes 1048600
  2.5 0.0 copy-start.1
  2.5 1.0 %copy-done.1 = bf16[1,128,2048]{2,1,0:T(8,128)(2,1)S(1)} copy-done((bf16[1,128,2048]{2,1,0:T(8,128)(2,1)S(1)}, bf16[1,128,2048]{2,1,0:T(8,128)(2,1)}, u32[]{:S(2)}) %copy-start.1) | copy-done | bytes 524312
  3.6 0.0 copy-start.2
  3.6 0.9 %copy-done.2 = bf16[1,128,1024]{2,1,0:T(8,128)(2,1)S(1)} copy-done((bf16[1,128,1024]{2,1,0:T(8,128)(2,1)S(1)}, bf16[1,128,1024]{2,1,0:T(8,128)(2,1)}, u32[]{:S(2)}) %copy-start.2) | copy-done | bytes 262168
  4.5 0.0 copy-start.3
  4.5 0.9 %copy-done.3 = bf16[1,128,1024]{2,1,0:T(8,128)(2,1)S(1)} copy-done((bf16[1,128,1024]{2,1,0:T(8,128)(2,1)S(1)}, bf16[1,128,1024]{2,1,0:T(8,128)(2,1)}, u32[]{:S(2)}) %copy-start.3) | copy-done | bytes 262168
  5.5 80.4 %shard_map.84 = (bf16[128,1024]{1,0:T(8,128)(2,1)S(1)}, bf16[128,2048]{1,0:T(8,128)(2,1)S(1)}, bf16[128,1024]{1,0:T(8,128)(2,1)S(1)}, bf16[512,1024]{1,0:T(8,128)(2,1)S(1)}) custom-call(bf16[128,2048]{1,0:T(8,128)(2,1)S(1)} %bitcast.11, bf16[512,1024]{1,0:T(8,128)(2,1)S(1)} %copy-done, bf16[128,1024]{1,0:T(8,128)(2,1)S(1)} %bitcast.12, ...), custom_call_target="tpu_custom_call" | custom-call | flops 2147483648 | bytes 8388608 | tf_op jit(solution)/shard_map/pallas_call | solution.py:523
  85.9 1.6 %convert_element_type.15 = f32[512,1024]{1,0:T(8,128)} convert(bf16[512,1024]{1,0:T(8,128)(2,1)S(1)} %get-tuple-element.11) | non-fusion elementwise | flops 524288 | bytes 3145728 | tf_op jit(solution)/shard_map/convert_element_type | solution.py:542
  87.5 0.7 copy.12
  88.2 0.8 copy.13
  89.0 0.7 copy.14
  (1 shorter events, 0.0 us)
Async XLA Ops:
  1.3 1.2 %copy-start = (bf16[512,1024]{1,0:T(8,128)(2,1)S(1)}, bf16[512,1024]{1,0:T(8,128)(2,1)}, u32[]{:S(2)}) copy-start(bf16[512,1024]{1,0:T(8,128)(2,1)} %weight_hbm.1) | copy-start | bytes 3145732
  2.5 1.0 %copy-start.1 = (bf16[1,128,2048]{2,1,0:T(8,128)(2,1)S(1)}, bf16[1,128,2048]{2,1,0:T(8,128)(2,1)}, u32[]{:S(2)}) copy-start(bf16[1,128,2048]{2,1,0:T(8,128)(2,1)} %param.5) | copy-start | bytes 1572868
  3.6 0.9 %copy-start.2 = (bf16[1,128,1024]{2,1,0:T(8,128)(2,1)S(1)}, bf16[1,128,1024]{2,1,0:T(8,128)(2,1)}, u32[]{:S(2)}) copy-start(bf16[1,128,1024]{2,1,0:T(8,128)(2,1)} %param.7) | copy-start | bytes 786436
  4.5 0.9 %copy-start.3 = (bf16[1,128,1024]{2,1,0:T(8,128)(2,1)S(1)}, bf16[1,128,1024]{2,1,0:T(8,128)(2,1)}, u32[]{:S(2)}) copy-start(bf16[1,128,1024]{2,1,0:T(8,128)(2,1)} %param.9) | copy-start | bytes 786436

commit v4 on v3

--- a/solution.py
+++ b/solution.py
@@ -304,7 +304,7 @@
                         preferred_element_type=jnp.float32,
                     )
         if turn >= 2:
-            for kind, k in waiting[2 * (turn - 2):2 * (turn - 1)]:
+            for kind, k in waiting[3 * (turn - 2):3 * (turn - 1)]:
                 send_rows(kind, k)
 
     for h in range(n):

time: 90.6 us -> 88.1 us (0.972)
  Pallas kernels: 80.4 us -> 78.6 us
    pallas_call x1, Pallas kernels: 80.4 us -> 78.6 us  [local_by_heads(): pl.pallas_call(along_heads_kernel, out_shape=(jax.ShapeDtypeStruct((tok,...]
where the time goes in v4:
time: 88.1 us; the launch traced here: 87.8 us
  Pallas kernels  78.6 us (89%)
  local copies, waits for them, and re-layouts  6.37 us (7%)
  other arithmetic  2.24 us (3%)
    pallas_call x1, Pallas kernels, local_by_heads(): pl.pallas_call(along_heads_kernel, out_shape=(jax.ShapeDtypeStruct((tok,...  78.6 us
    unnamed x11, local copies, waits for them, and re-layouts  6.36 us

profile of v4, /device:TPU:0, one launch (start us, length us, event | category | flops | bytes accessed | tf_op | source)
XLA Modules:
  0.0 87.8 jit_solution(11799209103238401441)
XLA Ops:
  0.6 0.7 convert_bitcast_fusion
  1.3 0.0 copy-start
  1.3 1.2 %copy-done = bf16[512,1024]{1,0:T(8,128)(2,1)S(1)} copy-done((bf16[512,1024]{1,0:T(8,128)(2,1)S(1)}, bf16[512,1024]{1,0:T(8,128)(2,1)}, u32[]{:S(2)}) %copy-start) | copy-done | bytes 1048600
  2.5 0.0 copy-start.1
  2.5 1.0 %copy-done.1 = bf16[1,128,2048]{2,1,0:T(8,128)(2,1)S(1)} copy-done((bf16[1,128,2048]{2,1,0:T(8,128)(2,1)S(1)}, bf16[1,128,2048]{2,1,0:T(8,128)(2,1)}, u32[]{:S(2)}) %copy-start.1) | copy-done | bytes 524312
  3.6 0.0 copy-start.2
  3.6 0.9 %copy-done.2 = bf16[1,128,1024]{2,1,0:T(8,128)(2,1)S(1)} copy-done((bf16[1,128,1024]{2,1,0:T(8,128)(2,1)S(1)}, bf16[1,128,1024]{2,1,0:T(8,128)(2,1)}, u32[]{:S(2)}) %copy-start.2) | copy-done | bytes 262168
  4.5 0.0 copy-start.3
  4.5 0.9 %copy-done.3 = bf16[1,128,1024]{2,1,0:T(8,128)(2,1)S(1)} copy-done((bf16[1,128,1024]{2,1,0:T(8,128)(2,1)S(1)}, bf16[1,128,1024]{2,1,0:T(8,128)(2,1)}, u32[]{:S(2)}) %copy-start.3) | copy-done | bytes 262168
  5.5 78.6 %shard_map.84 = (bf16[128,1024]{1,0:T(8,128)(2,1)S(1)}, bf16[128,2048]{1,0:T(8,128)(2,1)S(1)}, bf16[128,1024]{1,0:T(8,128)(2,1)S(1)}, bf16[512,1024]{1,0:T(8,128)(2,1)S(1)}) custom-call(bf16[128,2048]{1,0:T(8,128)(2,1)S(1)} %bitcast.11, bf16[512,1024]{1,0:T(8,128)(2,1)S(1)} %copy-done, bf16[128,1024]{1,0:T(8,128)(2,1)S(1)} %bitcast.12, ...), custom_call_target="tpu_custom_call" | custom-call | flops 2147483648 | bytes 8388608 | tf_op jit(solution)/shard_map/pallas_call | solution.py:523
  84.1 1.6 %convert_element_type.15 = f32[512,1024]{1,0:T(8,128)} convert(bf16[512,1024]{1,0:T(8,128)(2,1)S(1)} %get-tuple-element.11) | non-fusion elementwise | flops 524288 | bytes 3145728 | tf_op jit(solution)/shard_map/convert_element_type | solution.py:542
  85.6 0.7 copy.12
  86.3 0.8 copy.13
  87.1 0.7 copy.14
  (1 shorter events, 0.0 us)
Async XLA Ops:
  1.3 1.2 %copy-start = (bf16[512,1024]{1,0:T(8,128)(2,1)S(1)}, bf16[512,1024]{1,0:T(8,128)(2,1)}, u32[]{:S(2)}) copy-start(bf16[512,1024]{1,0:T(8,128)(2,1)} %weight_hbm.1) | copy-start | bytes 3145732
  2.5 1.0 %copy-start.1 = (bf16[1,128,2048]{2,1,0:T(8,128)(2,1)S(1)}, bf16[1,128,2048]{2,1,0:T(8,128)(2,1)}, u32[]{:S(2)}) copy-start(bf16[1,128,2048]{2,1,0:T(8,128)(2,1)} %param.5) | copy-start | bytes 1572868
  3.6 0.9 %copy-start.2 = (bf16[1,128,1024]{2,1,0:T(8,128)(2,1)S(1)}, bf16[1,128,1024]{2,1,0:T(8,128)(2,1)}, u32[]{:S(2)}) copy-start(bf16[1,128,1024]{2,1,0:T(8,128)(2,1)} %param.7) | copy-start | bytes 786436
  4.5 0.9 %copy-start.3 = (bf16[1,128,1024]{2,1,0:T(8,128)(2,1)S(1)}, bf16[1,128,1024]{2,1,0:T(8,128)(2,1)}, u32[]{:S(2)}) copy-start(bf16[1,128,1024]{2,1,0:T(8,128)(2,1)} %param.9) | copy-start | bytes 786436
